TPU v7x, 32 devices: a whole 2x2x4 slice. The times are simulated.
32 devices in a mesh: orb: 4 (over x, core), dom: 8 (over z, y).
Axes of the slice: x: 2, y: 2, z: 4, core: 2. Of those that a mesh axis runs over, the one named last changes fastest.
Arguments:
- orbitals: float32 [768, 32, 8, 128], P('orb', 'dom'), may hold values from -6 to 6
- potential: float32 [32, 8, 128], P('dom'), may hold values from -1 to 3
- prev_gradient: float32 [768, 32, 8, 128], P('orb', 'dom'), may hold values from -24 to 24
- prev_direction: float32 [768, 32, 8, 128], P('orb', 'dom'), may hold values from -24 to 24
Outputs:
- new_orbitals: float32 [768, 32, 8, 128], P('orb', 'dom')
- new_direction: float32 [768, 32, 8, 128], P('orb', 'dom')
- gradient: float32 [768, 32, 8, 128], P('orb', 'dom')
All inputs are finite; a program needn't handle non-finite values.
Results may differ from a plain program's by a relative error of at most 0.0002.
Values sent between devices are 32-bit elements; how exact they have to be, the bound alone decides.
A program may use at most 128 MiB of HBM per device.

v0:
```python
import jax
import jax.numpy as jnp
from jax import lax
from jax.sharding import PartitionSpec as P

coeffs = (-205.0 / 72.0, 8.0 / 5.0, -1.0 / 5.0, 8.0 / 315.0, -1.0 / 560.0)
step_length = 0.05


def padded_2(cells, sides, width):
    for axis, dim in sides:
        count = lax.axis_size(axis)
        ends = count - 1
        head = lax.slice_in_dim(cells, 0, width, axis=dim)
        tail = lax.slice_in_dim(cells, cells.shape[dim] - width, cells.shape[dim], axis=dim)
        cells = jnp.concatenate(
            [
                lax.ppermute(tail, axis, [(i, (i + 1) % count) for i in range(ends)]),
                cells,
                lax.ppermute(head, axis, [((i + 1) % count, i) for i in range(ends)]),
            ],
            axis=dim,
        )
    return cells


def laplace(padded, planes, lines, columns):
    center = padded[:, 4 : 4 + planes, 4 : 4 + lines, 4 : 4 + columns]
    total = 3.0 * coeffs[0] * center
    for offset in range(1, 5):
        total = total + coeffs[offset] * (
            padded[:, 4 + offset : 4 + offset + planes, 4 : 4 + lines, 4 : 4 + columns]
            + padded[:, 4 - offset : 4 - offset + planes, 4 : 4 + lines, 4 : 4 + columns]
        )
        total = total + coeffs[offset] * (
            padded[:, 4 : 4 + planes, 4 + offset : 4 + offset + lines, 4 : 4 + columns]
            + padded[:, 4 : 4 + planes, 4 - offset : 4 - offset + lines, 4 : 4 + columns]
        )
        total = total + coeffs[offset] * (
            padded[:, 4 : 4 + planes, 4 : 4 + lines, 4 + offset : 4 + offset + columns]
            + padded[:, 4 : 4 + planes, 4 : 4 + lines, 4 - offset : 4 - offset + columns]
        )
    return total


def highdot(left, right):
    return jnp.dot(left, right, precision=lax.Precision.HIGHEST, preferred_element_type=jnp.float32)


def on_device(orbitals, potential, prev_gradient, prev_direction):
    block = orbitals.shape[0]
    extended = padded_2(orbitals, (("dom", 1),), 4)
    padded = jnp.pad(extended, ((0, 0), (0, 0), (4, 4), (4, 4)))
    lap = laplace(padded, orbitals.shape[1], orbitals.shape[2], orbitals.shape[3])
    image = -0.5 * lap + potential[None] * orbitals
    cmat = orbitals.reshape(block, -1)
    hmat_rows = image.reshape(block, -1)
    cells = cmat.shape[1] * lax.axis_size("dom")
    all_orbs, all_images = (
        lax.all_gather(cmat, "orb", axis=0, tiled=True),
        lax.all_gather(hmat_rows, "orb", axis=0, tiled=True),
    )
    correlation, hamilton = lax.psum(
        (highdot(all_orbs, cmat.T), highdot(all_orbs, hmat_rows.T)), "dom"
    )
    correlation = correlation / cells
    hamilton = hamilton / cells
    grad = (
        4.0 * hmat_rows
        - 2.0 * highdot(correlation.T, all_images)
        - 2.0 * highdot(hamilton.T, all_orbs)
    )
    grad = grad.reshape(orbitals.shape)
    both, cross, before = lax.psum(
        (
            jnp.sum(grad * grad),
            jnp.sum(grad * prev_gradient),
            jnp.sum(prev_gradient * prev_gradient),
        ),
        ("orb", "dom"),
    )
    beta = (both - cross) / before
    direction = -grad + beta * prev_direction
    return (orbitals + step_length * direction, direction, grad)


def solution(mesh):
    in_specs = (
        P("orb", "dom", None, None),
        P("dom", None, None),
        P("orb", "dom", None, None),
        P("orb", "dom", None, None),
    )
    out_specs = (
        P("orb", "dom", None, None),
        P("orb", "dom", None, None),
        P("orb", "dom", None, None),
    )
    return jax.shard_map(
        on_device, mesh=mesh, in_specs=in_specs, out_specs=out_specs, check_vma=False
    )
```

profile of v0, /device:TPU:0, one launch (start us, length us, event | category | flops | bytes accessed | tf_op | source)
XLA Modules:
  0.0 541.8 jit_solution(9005797388195994688)
XLA Ops:
  7.2 0.0 all-gather.3.cloned.1.call-start
  7.2 6.3 %copy.16 = f32[24,8,32,128]{3,1,2,0:T(8,128)} copy(f32[24,8,32,128]{3,2,1,0:T(8,128)} %bitcast.23) | data formatting | bytes 6291456
  13.5 0.0 copy-start.1
  13.5 0.0 all-gather.3.cloned.1.call-update
  13.5 0.0 all-reduce.5.cloned.1.call-start
  13.6 1.8 copy-done.1
  15.4 5.1 collective-permute-start.1
  20.4 1.5 collective-permute-start
  21.9 133.1 %collective-permute-done.1 = f32[192,4,8,128]{3,2,1,0:T(8,128)S(1)} collective-permute-done((f32[192,4,8,128]{3,2,1,0:T(8,128)S(1)}, f32[192,4,8,128]{3,2,1,0:T(8,128)S(1)}, u32[]{:S(2)}, u32[]{:S(2)}) %collective-permute-start.1) | collective-permute-done | bytes 3145760 | tf_op jit(solution)/shard_map/ppermute | solution.py:18
  155.0 0.0 copy-start.3
  155.0 0.4 constant_dynamic-update-slice_fusion.3
  155.4 0.9 constant_dynamic-update-slice_fusion.1
  156.4 0.0 copy-start.6
  156.4 0.0 collective-permute-done
  156.4 0.0 copy-start.4
  156.4 0.4 constant_dynamic-update-slice_fusion
  156.9 0.9 copy-done.3
  157.7 0.4 copy-done.4
  158.1 0.0 copy-start.7
  158.1 0.0 copy-start.10
  158.1 17.8 %select_maximum_fusion = f32[192,12,16,136]{3,2,1,0:T(8,128)} fusion(f32[192,4,8,128]{3,2,1,0:T(8,128)S(1)} %collective-permute-done, f32[192,4,8,128]{3,2,1,0:T(8,128)S(1)} %copy-done.1, f32[192,4,8,128]{3,2,1,0:T(8,128)S(1)} %collective-permute-done.1), kind=kLoop, calls=%fused_computation.4 | loop fusion | flops 75202560 | bytes 29491200 | tf_op jit(solution)/shard_map/concatenate | solution.py:16
  175.9 0.0 copy-done.6
  175.9 0.0 copy-done.7
  175.9 0.0 copy-done.10
  175.9 75.9 %fusion.8 = f32[192,4,8,128]{3,2,1,0:T(8,128)} fusion(f32[192,12,16,136]{3,2,1,0:T(8,128)} %select_maximum_fusion, f32[192,8,8,128]{3,2,1,0:T(8,128)} %copy-done.6, f32[192,8,8,128]{3,2,1,0:T(8,128)} %copy-done.7, f32[192,4,8,128]{3,2,1,0:T(8,128)S(1)} %copy-done.1, f32[192,4,8,128]{3,2,1,0:T(8,128)} %copy-done.4, f32[192,4,8,128]{3,2,1,0:T(8,128)} %copy-done.3, ...), kind=kLoop, calls=%fused_computation.19 | loop fusion | flops 31457280 | bytes 81805312 | tf_op jit(solution)/shard_map/add | solution.py:55
  251.8 0.0 all-gather.3.cloned.1.call-done
  251.8 0.0 copy-start
  251.8 0.0 copy-start.2
  251.8 19.0 %fusion.36 = f32[768,192]{1,0:T(8,128)} fusion(f32[768,4096]{1,0:T(8,128)} %all-gather.3.cloned.1.call-done, f32[24,8,32,128]{3,2,1,0:T(8,128)S(1)} %bitcast.24), kind=kOutput, calls=%fused_computation.67 | convolution fusion | flops 7247757312 | bytes 16318464 | tf_op jit(solution)/shard_map/dot_general | solution.py:47
  270.9 0.0 copy-done
  270.9 0.0 copy-done.2
  270.9 11.2 %convolution_bitcast_fusion = f32[768,192]{1,0:T(8,128)} fusion(f32[768,4096]{1,0:T(8,128)S(1)} %copy-done, f32[24,8,32,128]{3,2,1,0:T(8,128)S(1)} %bitcast.27), kind=kOutput, calls=%fused_computation.56 | convolution fusion | flops 7247757312 | bytes 16318464 | tf_op jit(solution)/shard_map/dot_general | solution.py:47
  282.1 0.0 all-reduce.5.cloned.1.call-update
  282.1 0.0 all-gather.5.cloned.1.call-start
  282.2 6.3 %copy.17 = f32[24,8,32,128]{3,1,2,0:T(8,128)} copy(f32[24,8,32,128]{3,2,1,0:T(8,128)} %bitcast.25) | data formatting | bytes 6291456
  288.5 0.0 all-gather.5.cloned.1.call-update
  288.5 84.3 %all-reduce.5.cloned.1.call-done = (f32[768,192]{1,0:T(8,128)}, f32[768,192]{1,0:T(8,128)}) async-done(((f32[768,192]{1,0:T(8,128)}, f32[768,192]{1,0:T(8,128)}), (f32[768,192]{1,0:T(8,128)}, f32[768,192]{1,0:T(8,128)})) %all-reduce.5.cloned.1.call-update) | async-done | bytes 1179664 | tf_op jit(solution)/shard_map/psum | solution.py:63
  372.8 83.6 %all-gather.5.cloned.1.call-done = f32[768,4096]{1,0:T(8,128)} async-done(((f32[192,4096]{1,0:T(8,128)}), f32[768,4096]{1,0:T(8,128)}) %all-gather.5.cloned.1.call-update) | async-done | bytes 12582928 | tf_op jit(solution)/shard_map/all_gather | solution.py:61
  456.4 0.0 copy-start.9
  456.4 13.4 %fusion.3 = f32[192,4096]{1,0:T(8,128)S(1)} fusion(f32[768,4096]{1,0:T(8,128)} %all-gather.5.cloned.1.call-done, f32[768,192]{1,0:T(8,128)} %get-tuple-element.8, f32[24,8,32,128]{3,2,1,0:T(8,128)} %bitcast.26), kind=kOutput, calls=%fused_computation.11 | convolution fusion | flops 7250264064 | bytes 19464192 | tf_op jit(solution)/shard_map/dot_general | solution.py:47
  469.8 0.0 copy-done.9
  469.8 12.4 %multiply_reduce_fusion.2 = (f32[]{:T(128)}, f32[192,4096]{1,0:T(8,128)S(1)}) fusion(f32[192,4096]{1,0:T(8,128)S(1)} %fusion.3, f32[768,4096]{1,0:T(8,128)} %all-gather.3.cloned.1.call-done, f32[768,192]{1,0:T(8,128)S(1)} %copy-done.9), kind=kOutput, calls=%fused_computation.55 | convolution fusion | flops 7251050496 | bytes 19464196 | tf_op jit(solution)/shard_map/dot_general | solution.py:47
  482.2 0.0 copy-start.8
  482.2 0.5 copy.9
  482.8 0.0 copy-start.5
  482.8 2.2 copy-done.8
  485.0 1.8 multiply_reduce_fusion
  486.8 0.0 copy-done.5
  486.8 39.6 %all-reduce.1 = (f32[]{:T(128)}, f32[]{:T(128)}, f32[]{:T(128)}) all-reduce(f32[]{:T(128)} %get-tuple-element.14, f32[]{:T(128)} %get-tuple-element.4, f32[]{:T(128)} %get-tuple-element.3), channel_id=1, replica_groups=mesh['orb'=4,'dom'=8] {'orb','dom'}, use_global_device_ids=true, to_apply=%region_3.4 | all-reduce | flops 3 | bytes 24 | tf_op jit(solution)/shard_map/psum | solution.py:74
  528.4 6.7 %multiply_add_fusion = (f32[192,4,8,128]{3,2,1,0:T(8,128)}, f32[192,4,8,128]{3,2,1,0:T(8,128)}) fusion(f32[192,4,8,128]{3,2,1,0:T(8,128)S(1)} %copy-done.1, f32[192,4,8,128]{3,2,1,0:T(8,128)} %param.7, f32[]{:T(128)S(6)} %div.11, f32[192,4,8,128]{3,2,1,0:T(8,128)} %bitcast.29), kind=kLoop, calls=%fused_computation.51 | loop fusion | flops 3932160 | bytes 15728644 | tf_op jit(solution)/shard_map/add | solution.py:84
Async XLA Ops:
  7.2 244.6 %all-gather.3.cloned.1.call-start = ((), (), s32[]{:S(2)}) async-start(), calls=%async_computation | async-start | bytes 15728640 | tf_op jit(solution)/shard_map/all_gather | solution.py:60
  13.5 1.9 copy-start.1
  13.5 359.3 %all-reduce.5.cloned.1.call-start = ((), (), s32[]{:S(2)}) async-start(), calls=%async_computation.2 | async-start | bytes 3145728 | tf_op jit(solution)/shard_map/psum | solution.py:63
  15.4 139.6 %collective-permute-start.1 = (f32[192,4,8,128]{3,2,1,0:T(8,128)S(1)}, f32[192,4,8,128]{3,2,1,0:T(8,128)S(1)}, u32[]{:S(2)}, u32[]{:S(2)}) collective-permute-start(f32[192,4,8,128]{3,2,1,0:T(8,128)S(1)} %copy-done.1), channel_id=1, source_target_pairs={{0,1},{1,2},{2,3},{3,4},{4,5},{5,6},{6,7},{8,9},{9,10},{10,11},{11... | collective-permute-start | bytes 9437192 | tf_op jit(solution)/shard_map/ppermute | solution.py:18
  20.4 136.0 %collective-permute-start = (f32[192,4,8,128]{3,2,1,0:T(8,128)S(1)}, f32[192,4,8,128]{3,2,1,0:T(8,128)S(1)}, u32[]{:S(2)}, u32[]{:S(2)}) collective-permute-start(f32[192,4,8,128]{3,2,1,0:T(8,128)S(1)} %copy-done.1), channel_id=1, source_target_pairs={{1,0},{2,1},{3,2},{4,3},{5,4},{6,5},{7,6},{9,8},{10,9},{11,10},{12... | collective-permute-start | bytes 9437192 | tf_op jit(solution)/shard_map/ppermute | solution.py:20
  155.0 2.7 copy-start.3
  156.4 19.5 %copy-start.6 = (f32[192,8,8,128]{3,2,1,0:T(8,128)}, f32[192,8,8,128]{3,2,1,0:T(8,128)S(1)}, u32[]{:S(2)}) copy-start(f32[192,8,8,128]{3,2,1,0:T(8,128)S(1)} %get-tuple-element.13) | copy-start | bytes 18874372
  156.4 1.7 copy-start.4
  158.1 17.8 %copy-start.7 = (f32[192,8,8,128]{3,2,1,0:T(8,128)}, f32[192,8,8,128]{3,2,1,0:T(8,128)S(1)}, u32[]{:S(2)}) copy-start(f32[192,8,8,128]{3,2,1,0:T(8,128)S(1)} %constant_dynamic-update-slice_fusion) | copy-start | bytes 18874372
  158.1 17.8 %copy-start.10 = (f32[4,8,128]{2,1,0:T(8,128)S(1)}, f32[4,8,128]{2,1,0:T(8,128)}, u32[]{:S(2)}) copy-start(f32[4,8,128]{2,1,0:T(8,128)} %param.5) | copy-start | bytes 49156
  251.8 19.1 %copy-start = (f32[768,4096]{1,0:T(8,128)S(1)}, f32[768,4096]{1,0:T(8,128)}, u32[]{:S(2)}) copy-start(f32[768,4096]{1,0:T(8,128)} %all-gather.3.cloned.1.call-done) | copy-start | bytes 37748740
  251.8 19.1 %copy-start.2 = (f32[192,4,8,128]{3,2,1,0:T(8,128)S(1)}, f32[192,4,8,128]{3,2,1,0:T(8,128)}, u32[]{:S(2)}) copy-start(f32[192,4,8,128]{3,2,1,0:T(8,128)} %fusion.8) | copy-start | bytes 9437188
  282.1 174.3 %all-gather.5.cloned.1.call-start = ((), (), s32[]{:S(2)}) async-start(), calls=%async_computation.1 | async-start | bytes 15728640 | tf_op jit(solution)/shard_map/all_gather | solution.py:61
  456.4 13.4 %copy-start.9 = (f32[768,192]{1,0:T(8,128)S(1)}, f32[768,192]{1,0:T(8,128)}, u32[]{:S(2)}) copy-start(f32[768,192]{1,0:T(8,128)} %get-tuple-element.9) | copy-start | bytes 1769476
  482.2 2.8 copy-start.8
  482.8 4.1 copy-start.5
Sparse Core Ops, SparseCore 0:
  13.6 84.7 all-gather.2
  282.3 90.4 all-reduce.4
  374.9 81.4 all-gather.4
where the time goes:
time: 546 us; the launch traced here: 542 us
  waiting for transfers between devices  301 us (55%)
  other arithmetic  102 us (19%)
  matrix products  56 us (10%)
  blocking collectives  39.6 us (7%)
  local copies, waits for them, and re-layouts  20.2 us (4%)
  between operations  16 us (3%)
  starting transfers between devices  6.65 us (1%)
    ppermute x1, waiting for transfers between devices, padded_2(): lax.ppermute(tail, axis, [(i, (i + 1) % count) for i in range(ends)])  133 us
    psum x1, waiting for transfers between devices, on_device(): lax.psum((highdot(all_orbs, cmat.T), highdot(all_orbs, hmat_rows.T)), 'dom')  84.3 us
    all_gather x1, waiting for transfers between devices, on_device(): lax.all_gather(hmat_rows, 'orb', axis=0, tiled=True)  83.6 us
    add x1, other arithmetic, on_device(): image = -0.5 * lap + potential[None] * orbitals  75.9 us
    dot_general x4, matrix products, highdot(): jnp.dot(left, right, precision=lax.Precision.HIGHEST, preferred_element_t...  56 us
    psum x1, blocking collectives, on_device(): lax.psum((jnp.sum(grad * grad), jnp.sum(grad * prev_gradient), jnp.sum(pr...  39.6 us
    unnamed x27, local copies, waits for them, and re-layouts  19.8 us
    concatenate x1, other arithmetic, padded_2(): jnp.concatenate([lax.ppermute(tail, axis, [(i, (i + 1) % count) for i in...  17.8 us
  transfers between devices with their start and end apart: 5, of which 3 were waited for; matrix products, arithmetic and copies ran while one was open for 19% of the time, Pallas kernels for 0%

commit v1 on v0

v1 whole, which is shorter than its diff:
```python
import functools

import jax
import jax.numpy as jnp
from jax import lax
from jax.experimental import pallas as pl
from jax.experimental.pallas import tpu as pltpu
from jax.sharding import PartitionSpec as P

coeffs = (-205.0 / 72.0, 8.0 / 5.0, -1.0 / 5.0, 8.0 / 315.0, -1.0 / 560.0)
step_length = 0.05
width = 4
MESH = pl.DeviceIdType.MESH
NT = (((1,), (1,)), ((), ()))
NN = (((1,), (0,)), ((), ()))


def split(value):
    high = value.astype(jnp.bfloat16)
    return high, (value - high.astype(jnp.float32)).astype(jnp.bfloat16)


def dot3(left, right, dims):
    def dot(a, b):
        return lax.dot_general(a, b, dims, preferred_element_type=jnp.float32)

    return dot(left[0], right[0]) + (dot(left[0], right[1]) + dot(left[1], right[0]))


def kernel(
    cfg, c_hbm, pot, pg_hbm, grad_out, stat_out,
    orbs, images, halo, pg, part, inbox, full, acc, near, far,
    local_sem, halo_s, halo_r, c_s, c_r, cf_s, cf_r, i_s, i_r, if_s, if_r,
    rs_s, rs_r, ag_s, ag_r, n_s, n_r, f_s, f_r,
):
    no, nd, planes, lines, block, chunks = cfg
    rows = planes * lines
    edge = width * lines
    size = block // chunks
    nx = no // 2
    count = no * block
    share = block // nd
    cells = rows * 128 * nd
    o, d = lax.axis_index("orb"), lax.axis_index("dom")
    core = lax.rem(o, 2)
    column = o // 2
    mate = column * 2 + (1 - core)
    tos = [lax.rem(column + j, nx) * 2 + core for j in range(1, nx)]
    froms = [lax.rem(column - j + nx, nx) * 2 + core for j in range(1, nx)]

    load = pltpu.make_async_copy(c_hbm, orbs.at[o], local_sem.at[0])
    load.start()
    for r in range(rows):
        pltpu.make_async_copy(
            pg_hbm.at[:, r // lines, r % lines, :], pg.at[r], local_sem.at[1]
        ).start()

    barrier = pltpu.get_barrier_semaphore()
    for j in range(1, no):
        pl.semaphore_signal(barrier, inc=1, device_id=(lax.rem(o + j, no), d), device_id_type=MESH)
    for j in range(1, nd):
        pl.semaphore_signal(barrier, inc=1, device_id=(o, lax.rem(d + j, nd)), device_id_type=MESH)
    load.wait()
    pl.semaphore_wait(barrier, no + nd - 2)

    def cut(c):
        return pl.ds(pl.multiple_of(c * size, 8), size)

    def remote(src, dst, send, recv, device):
        return pltpu.make_async_remote_copy(
            src_ref=src, dst_ref=dst, send_sem=send, recv_sem=recv, device_id=device, device_id_type=MESH
        )

    def up(c):
        return remote(
            orbs.at[o, pl.ds(rows - edge, edge), cut(c), :], halo.at[0, :, cut(c), :],
            halo_s.at[0, c], halo_r.at[0, c], (o, lax.rem(d + 1, nd)),
        )

    def down(c):
        return remote(
            orbs.at[o, pl.ds(0, edge), cut(c), :], halo.at[1, :, cut(c), :],
            halo_s.at[1, c], halo_r.at[1, c], (o, lax.rem(d + nd - 1, nd)),
        )

    def start_halo(c):
        @pl.when(d < nd - 1)
        def _():
            up(c).start()

        @pl.when(d > 0)
        def _():
            down(c).start()

    def spread(buf, send, recv, c, j):
        to = mate if j == 0 else tos[j - 1]
        ref = buf.at[o, :, cut(c), :]
        return remote(ref, ref, send.at[j, c], recv.at[j, c], (to, d))

    def forward(buf, send, recv, c, j):
        ref = buf.at[froms[j - 1], :, cut(c), :]
        return remote(ref, ref, send.at[j - 1, c], recv.at[j - 1, c], (mate, d))

    def start_spread(buf, send, recv, c):
        for j in list(range(1, nx)) + [0]:
            spread(buf, send, recv, c, j).start()

    def pass_on(buf, recv, send_f, recv_f, c):
        for j in range(1, nx):
            spread(buf, recv, recv, c, j).wait_recv()
            forward(buf, send_f, recv_f, c, j).start()

    start_halo(0)
    if chunks > 1:
        start_halo(1)
    for c in range(chunks):
        start_spread(orbs, c_s, c_r, c)

    @pl.when(d == 0)
    def _():
        halo[0] = jnp.zeros(halo.shape[1:], jnp.float32)

    @pl.when(d == nd - 1)
    def _():
        halo[1] = jnp.zeros(halo.shape[1:], jnp.float32)

    away = jnp.abs(
        lax.broadcasted_iota(jnp.int32, (128, 128), 0) - lax.broadcasted_iota(jnp.int32, (128, 128), 1)
    )
    band = jnp.zeros((128, 128), jnp.float32)
    for k in range(1, width + 1):
        band = jnp.where(away == k, -0.5 * coeffs[k], band)
    band = split(band)

    def stencil(c):
        at = cut(c)

        def line(p, y):
            if p < 0:
                return halo[0, (p + width) * lines + y, at, :]
            if p >= planes:
                return halo[1, (p - planes) * lines + y, at, :]
            return orbs[o, p * lines + y, at, :]

        for p in range(planes):
            mid = orbs[o, pl.ds(p * lines, lines), at, :]
            along = dot3(split(mid.reshape(lines * size, 128)), band, NN).reshape(lines, size, 128)
            for y in range(lines):
                total = along[y] + (pot[p * lines + y] - 1.5 * coeffs[0]) * line(p, y)
                for k in range(1, width + 1):
                    near_ = line(p + k, y) + line(p - k, y)
                    if y + k < lines:
                        near_ = near_ + line(p, y + k)
                    if y - k >= 0:
                        near_ = near_ + line(p, y - k)
                    total = total + (-0.5 * coeffs[k]) * near_
                images[o, p * lines + y, at, :] = total

    def step(c):
        @pl.when(d > 0)
        def _():
            up(c).wait_recv()

        @pl.when(d < nd - 1)
        def _():
            down(c).wait_recv()

        stencil(c)
        start_spread(images, i_s, i_r, c)
        pass_on(orbs, c_r, cf_s, cf_r, c)

    group = next(g for g in (4, 2, 1) if rows % g == 0)

    def gathered(buf, r):
        return jnp.concatenate(
            [jnp.concatenate([buf[s, r * group + i] for i in range(group)], axis=1) for s in range(no)], axis=0
        )

    def mine(buf, r):
        return jnp.concatenate([buf[o, r * group + i] for i in range(group)], axis=1)

    def overlaps(buf, slot):
        acc[...] = jnp.zeros(acc.shape, jnp.float32)

        def body(r, carry):
            acc[...] += dot3(split(mine(buf, r)), split(gathered(orbs, r)), NT)
            return carry

        lax.fori_loop(0, rows // group, body, 0)
        for e in range(nd):
            part[slot, e] = acc[e * share : (e + 1) * share, :]

    def scatter(slot, j):
        e = lax.rem(d + j, nd)
        return remote(
            part.at[slot, e], inbox.at[slot, d], rs_s.at[slot, j - 1], rs_r.at[slot, j - 1], (o, e)
        )

    def share_out(slot, j):
        e = lax.rem(d + j, nd)
        ref = full.at[slot, d]
        return remote(ref, ref, ag_s.at[slot, j - 1], ag_r.at[slot, j - 1], (o, e))

    def reduce_start(slot):
        for j in range(1, nd):
            scatter(slot, j).start()
        inbox[slot, d] = part[slot, d]

    def reduce_mid(slot):
        for j in range(1, nd):
            scatter(slot, j).wait_recv()
        total = inbox[slot, 0]
        for e in range(1, nd):
            total = total + inbox[slot, e]
        full[slot, d] = total * (1.0 / cells)
        for j in range(1, nd):
            share_out(slot, j).start()

    def reduce_end(slot):
        for j in range(1, nd):
            share_out(slot, j).wait_recv()

    def early(c, carry):
        @pl.when(c + 2 < chunks)
        def _():
            start_halo(c + 2)

        step(c)

        @pl.when(c > 0)
        def _():
            pass_on(images, i_r, if_s, if_r, c - 1)

        return carry

    lax.fori_loop(0, chunks - 1, early, 0)
    last = chunks - 1
    pass_on(orbs, c_r, cf_s, cf_r, last)

    def arrive(c, carry):
        spread(orbs, c_s, c_r, c, 0).wait_recv()
        for j in range(1, nx):
            forward(orbs, cf_s, cf_r, c, j).wait_recv()
        return carry

    lax.fori_loop(0, chunks, arrive, 0)
    overlaps(orbs, 0)
    reduce_start(0)

    @pl.when(d > 0)
    def _():
        up(last).wait_recv()

    @pl.when(d < nd - 1)
    def _():
        down(last).wait_recv()

    stencil(last)
    start_spread(images, i_s, i_r, last)
    if chunks > 1:
        pass_on(images, i_r, if_s, if_r, last - 1)
    reduce_mid(0)
    overlaps(images, 1)
    reduce_start(1)
    pass_on(images, i_r, if_s, if_r, last)
    reduce_end(0)
    reduce_mid(1)

    def arrive_images(c, carry):
        spread(images, i_s, i_r, c, 0).wait_recv()
        for j in range(1, nx):
            forward(images, if_s, if_r, c, j).wait_recv()
        return carry

    lax.fori_loop(0, chunks, arrive_images, 0)
    reduce_end(1)
    pltpu.make_async_copy(pg, pg, local_sem.at[1]).wait()

    def matrix(slot):
        return jnp.concatenate([full[slot, e] for e in range(nd)], axis=0)

    def fold(value):
        return jnp.sum(value.reshape(block // 8, 8, 128), axis=0)

    correlation, hamilton = split(matrix(0)), split(matrix(1))

    def gradient(r, sums):
        mixed = dot3(correlation, split(gathered(images, r)), NN) + dot3(hamilton, split(gathered(orbs, r)), NN)
        both, cross, before = sums
        for i in range(group):
            at = r * group + i
            grad = 4.0 * images[o, at] - 2.0 * mixed[:, i * 128 : (i + 1) * 128]
            grad_out[at] = grad
            old = pg[at]
            both = both + fold(grad * grad)
            cross = cross + fold(grad * old)
            before = before + fold(old * old)
        return both, cross, before

    zero = jnp.zeros((8, 128), jnp.float32)
    sums = lax.fori_loop(0, rows // group, gradient, (zero, zero, zero))

    near[o] = jnp.concatenate(
        [jnp.sum(s, axis=0, keepdims=True) for s in sums] + [jnp.zeros((5, 128), jnp.float32)], axis=0
    )

    def tell(buf, at, j, send, recv, device):
        return remote(buf.at[at], buf.at[at], send.at[j - 1], recv.at[j - 1], device)

    def near_copy(j):
        return tell(near, o, j, n_s, n_r, (lax.rem(o + j, no), d))

    def far_copy(j):
        return tell(far, d, j, f_s, f_r, (o, lax.rem(d + j, nd)))

    for j in range(1, no):
        near_copy(j).start()
    for j in range(1, no):
        near_copy(j).wait_recv()
    total = near[0]
    for s in range(1, no):
        total = total + near[s]
    far[d] = total
    for j in range(1, nd):
        far_copy(j).start()
    for j in range(1, nd):
        far_copy(j).wait_recv()
    total = far[0]
    for s in range(1, nd):
        total = total + far[s]
    stat_out[...] = total

    def drain(c, carry):
        @pl.when(d < nd - 1)
        def _():
            up(c).wait_send()

        @pl.when(d > 0)
        def _():
            down(c).wait_send()

        for j in range(nx):
            spread(orbs, c_s, c_r, c, j).wait_send()
            spread(images, i_s, i_r, c, j).wait_send()
        for j in range(1, nx):
            forward(orbs, cf_s, cf_r, c, j).wait_send()
            forward(images, if_s, if_r, c, j).wait_send()
        return carry

    lax.fori_loop(0, chunks, drain, 0)
    for j in range(1, nd):
        for slot in range(2):
            scatter(slot, j).wait_send()
            share_out(slot, j).wait_send()
        far_copy(j).wait_send()
    for j in range(1, no):
        near_copy(j).wait_send()


def on_device(no, nd, orbitals, potential, prev_gradient, prev_direction):
    block, planes, lines, columns = orbitals.shape
    rows = planes * lines
    chunks = next(n for n in (6, 4, 3, 2, 1) if block % (8 * n) == 0)
    nx = no // 2
    share = block // nd
    f32 = jnp.float32
    dma = pltpu.SemaphoreType.DMA
    turned = orbitals.reshape(block, rows, columns).transpose(1, 0, 2)
    links = max(nx - 1, 1)
    grad, stats = pl.pallas_call(
        functools.partial(kernel, (no, nd, planes, lines, block, chunks)),
        out_shape=(
            jax.ShapeDtypeStruct((rows, block, columns), f32),
            jax.ShapeDtypeStruct((8, columns), f32),
        ),
        in_specs=[
            pl.BlockSpec(memory_space=pl.ANY),
            pl.BlockSpec(memory_space=pltpu.VMEM),
            pl.BlockSpec(memory_space=pl.ANY),
        ],
        out_specs=(pl.BlockSpec(memory_space=pltpu.VMEM), pl.BlockSpec(memory_space=pltpu.VMEM)),
        scratch_shapes=[
            pltpu.VMEM((no, rows, block, columns), f32),
            pltpu.VMEM((no, rows, block, columns), f32),
            pltpu.VMEM((2, width * lines, block, columns), f32),
            pltpu.VMEM((rows, block, columns), f32),
            pltpu.VMEM((2, nd, share, no * block), f32),
            pltpu.VMEM((2, nd, share, no * block), f32),
            pltpu.VMEM((2, nd, share, no * block), f32),
            pltpu.VMEM((block, no * block), f32),
            pltpu.VMEM((no, 8, columns), f32),
            pltpu.VMEM((nd, 8, columns), f32),
            dma((2,)),
            dma((2, chunks)), dma((2, chunks)),
            dma((nx, chunks)), dma((nx, chunks)), dma((links, chunks)), dma((links, chunks)),
            dma((nx, chunks)), dma((nx, chunks)), dma((links, chunks)), dma((links, chunks)),
            dma((2, nd - 1)), dma((2, nd - 1)), dma((2, nd - 1)), dma((2, nd - 1)),
            dma((no - 1,)), dma((no - 1,)), dma((nd - 1,)), dma((nd - 1,)),
        ],
        compiler_params=pltpu.CompilerParams(
            collective_id=0, has_side_effects=True, vmem_limit_bytes=60 * 1024 * 1024
        ),
    )(turned, potential.reshape(rows, 1, columns), prev_gradient)
    grad = grad.transpose(1, 0, 2).reshape(orbitals.shape)
    both, cross, before = jnp.sum(stats[0]), jnp.sum(stats[1]), jnp.sum(stats[2])
    beta = (both - cross) / before
    direction = -grad + beta * prev_direction
    return (orbitals + step_length * direction, direction, grad)


def solution(mesh):
    spec = P("orb", "dom", None, None)
    return jax.shard_map(
        functools.partial(on_device, mesh.shape["orb"], mesh.shape["dom"]),
        mesh=mesh,
        in_specs=(spec, P("dom", None, None), spec, spec),
        out_specs=(spec, spec, spec),
        check_vma=False,
    )
```

time: 546 us -> 237 us (0.43)
  waiting for transfers between devices: 301 us -> 0 us
  Pallas kernels: 0 us -> 219 us
  other arithmetic: 102 us -> 10.2 us
  matrix products: 56 us -> 0 us
  blocking collectives: 39.6 us -> 0 us
  local copies, waits for them, and re-layouts: 20.2 us -> 5.38 us
  between operations: 16 us -> 2.63 us
  starting transfers between devices: 6.65 us -> 0 us
    pallas_call x0 -> x1, Pallas kernels: none -> 219 us  [on_device(): pl.pallas_call(functools.partial(kernel, (no, nd, planes, lines, block, c...]
    ppermute x2 -> x0, waiting for transfers between devices: 133 us -> none  [the longest x1 133 us: padded_2(): lax.ppermute(tail, axis, [(i, (i + 1) % count) for i in range(ends)])]
    psum x1 -> x0, waiting for transfers between devices: 84.3 us -> none  [on_device(): lax.psum((highdot(all_orbs, cmat.T), highdot(all_orbs, hmat_rows.T)), 'dom')]
    all_gather x2 -> x0, waiting for transfers between devices: 83.7 us -> none  [the longest x1 83.6 us: on_device(): lax.all_gather(hmat_rows, 'orb', axis=0, tiled=True)]
    add x1 -> x0, other arithmetic: 75.9 us -> none  [on_device(): image = -0.5 * lap + potential[None] * orbitals]
    dot_general x4 -> x0, matrix products: 56 us -> none  [highdot(): jnp.dot(left, right, precision=lax.Precision.HIGHEST, preferred_element_t...]
    psum x1 -> x0, blocking collectives: 39.6 us -> none  [on_device(): lax.psum((jnp.sum(grad * grad), jnp.sum(grad * prev_gradient), jnp.sum(pr...]
    concatenate x1 -> x0, other arithmetic: 17.8 us -> none  [padded_2(): jnp.concatenate([lax.ppermute(tail, axis, [(i, (i + 1) % count) for i in...]
  transfers between devices with their start and end apart: 5 -> 0, of which waited for: 3 -> 0; matrix products, arithmetic and copies ran while one was open for 19% -> 0% of each run, Pallas kernels for 0% -> 0%
where the time goes in v1:
time: 237 us
  Pallas kernels  219 us (92%)
  other arithmetic  10.2 us (4%)
  local copies, waits for them, and re-layouts  5.38 us (2%)
  between operations  2.63 us (1%)
    pallas_call x1, Pallas kernels, on_device(): pl.pallas_call(functools.partial(kernel, (no, nd, planes, lines, block, c...  219 us
    add x1, other arithmetic, on_device(): return (orbitals + step_length * direction, direction, grad)  8.81 us
    unnamed x3, local copies, waits for them, and re-layouts  5.38 us

profile of v1, /device:TPU:0, one launch (start us, length us, event | category | flops | bytes accessed | tf_op | source)
XLA Modules:
  0.0 237.2 jit_solution(13066396760327984840)
XLA Ops:
  0.6 5.4 %copy.7 = f32[192,4,8,128]{3,0,2,1:T(8,128)} copy(f32[192,4,8,128]{3,2,1,0:T(8,128)} %param.4) | data formatting | bytes 6291456 | tf_op args[0]
  6.0 0.0 copy-start
  6.0 218.9 %shard_map.67 = (f32[32,192,128]{2,1,0:T(8,128)}, f32[8,128]{1,0:T(8,128)}) custom-call(f32[32,192,128]{2,1,0:T(8,128)} %bitcast.7, f32[32,1,128]{2,1,0:T(1,128)} %bitcast.9, f32[192,4,8,128]{3,2,1,0:T(8,128)} %pg_hbm.1), custom_call_target="tpu_custom_call" | custom-call | tf_op jit(solution)/shard_map/pallas_call | solution.py:370
  224.9 1.4 slice_reduce_fusion
  228.3 0.0 copy-done
  228.3 8.8 %multiply_add_fusion = (f32[192,4,8,128]{3,2,1,0:T(8,128)}, f32[192,4,8,128]{3,2,1,0:T(8,128)}, f32[192,4,8,128]{3,2,1,0:T(8,128)}) fusion(f32[192,4,8,128]{3,2,1,0:T(8,128)S(1)} %copy-done, f32[192,4,8,128]{3,2,1,0:T(8,128)} %param.7, f32[]{:T(128)S(6)} %div.3, f32[192,4,8,128]{3,0,2,1:T(8,128)} %bitcast.8), kind=kLoop, calls=%fused_computation | loop fusion | flops 3932160 | bytes 18874372 | tf_op jit(solution)/shard_map/add | solution.py:408
Async XLA Ops:
  6.0 222.3 %copy-start = (f32[192,4,8,128]{3,2,1,0:T(8,128)S(1)}, f32[192,4,8,128]{3,2,1,0:T(8,128)}, u32[]{:S(2)}) copy-start(f32[192,4,8,128]{3,2,1,0:T(8,128)} %param.4) | copy-start | bytes 9437188

commit v2 on v1

--- a/solution.py
+++ b/solution.py
@@ -29,7 +29,7 @@
 
 def kernel(
     cfg, c_hbm, pot, pg_hbm, grad_out, stat_out,
-    orbs, images, halo, pg, part, inbox, full, acc, near, far,
+    orbs, images, halo, pg, part0, inbox0, full0, part1, inbox1, full1, acc, near, far,
     local_sem, halo_s, halo_r, c_s, c_r, cf_s, cf_r, i_s, i_r, if_s, if_r,
     rs_s, rs_r, ag_s, ag_r, n_s, n_r, f_s, f_r,
 ):
@@ -39,8 +39,10 @@
     size = block // chunks
     nx = no // 2
     count = no * block
-    share = block // nd
     cells = rows * 128 * nd
+    last = chunks - 1
+    heights = (block + last * size, size)
+    part, inbox, full = (part0, part1), (inbox0, inbox1), (full0, full1)
     o, d = lax.axis_index("orb"), lax.axis_index("dom")
     core = lax.rem(o, 2)
     column = o // 2
@@ -176,43 +178,51 @@
             [jnp.concatenate([buf[s, r * group + i] for i in range(group)], axis=1) for s in range(no)], axis=0
         )
 
-    def mine(buf, r):
-        return jnp.concatenate([buf[o, r * group + i] for i in range(group)], axis=1)
-
-    def overlaps(buf, slot):
-        acc[...] = jnp.zeros(acc.shape, jnp.float32)
+    def mine(buf, r, begin, end):
+        return jnp.concatenate([buf[o, r * group + i, begin:end, :] for i in range(group)], axis=1)
+
+    def overlaps(slot):
+        height = heights[slot]
+        share = height // nd
+        acc[0:height, :] = jnp.zeros((height, count), jnp.float32)
 
         def body(r, carry):
-            acc[...] += dot3(split(mine(buf, r)), split(gathered(orbs, r)), NT)
+            if slot == 1:
+                left = mine(images, r, last * size, block)
+            elif last == 0:
+                left = mine(orbs, r, 0, block)
+            else:
+                left = jnp.concatenate([mine(orbs, r, 0, block), mine(images, r, 0, last * size)], axis=0)
+            acc[0:height, :] += dot3(split(left), split(gathered(orbs, r)), NT)
             return carry
 
         lax.fori_loop(0, rows // group, body, 0)
         for e in range(nd):
-            part[slot, e] = acc[e * share : (e + 1) * share, :]
+            part[slot][e] = acc[e * share : (e + 1) * share, :]
 
     def scatter(slot, j):
         e = lax.rem(d + j, nd)
         return remote(
-            part.at[slot, e], inbox.at[slot, d], rs_s.at[slot, j - 1], rs_r.at[slot, j - 1], (o, e)
+            part[slot].at[e], inbox[slot].at[d], rs_s.at[slot, j - 1], rs_r.at[slot, j - 1], (o, e)
         )
 
     def share_out(slot, j):
         e = lax.rem(d + j, nd)
-        ref = full.at[slot, d]
+        ref = full[slot].at[d]
         return remote(ref, ref, ag_s.at[slot, j - 1], ag_r.at[slot, j - 1], (o, e))
 
     def reduce_start(slot):
         for j in range(1, nd):
             scatter(slot, j).start()
-        inbox[slot, d] = part[slot, d]
+        inbox[slot][d] = part[slot][d]
 
     def reduce_mid(slot):
         for j in range(1, nd):
             scatter(slot, j).wait_recv()
-        total = inbox[slot, 0]
+        total = inbox[slot][0]
         for e in range(1, nd):
-            total = total + inbox[slot, e]
-        full[slot, d] = total * (1.0 / cells)
+            total = total + inbox[slot][e]
+        full[slot][d] = total * (1.0 / cells)
         for j in range(1, nd):
             share_out(slot, j).start()
 
@@ -234,7 +244,6 @@
         return carry
 
     lax.fori_loop(0, chunks - 1, early, 0)
-    last = chunks - 1
     pass_on(orbs, c_r, cf_s, cf_r, last)
 
     def arrive(c, carry):
@@ -244,7 +253,7 @@
         return carry
 
     lax.fori_loop(0, chunks, arrive, 0)
-    overlaps(orbs, 0)
+    overlaps(0)
     reduce_start(0)
 
     @pl.when(d > 0)
@@ -257,14 +266,14 @@
 
     stencil(last)
     start_spread(images, i_s, i_r, last)
+    overlaps(1)
+    reduce_start(1)
+    reduce_mid(0)
+    reduce_mid(1)
     if chunks > 1:
         pass_on(images, i_r, if_s, if_r, last - 1)
-    reduce_mid(0)
-    overlaps(images, 1)
-    reduce_start(1)
     pass_on(images, i_r, if_s, if_r, last)
     reduce_end(0)
-    reduce_mid(1)
 
     def arrive_images(c, carry):
         spread(images, i_s, i_r, c, 0).wait_recv()
@@ -277,12 +286,14 @@
     pltpu.make_async_copy(pg, pg, local_sem.at[1]).wait()
 
     def matrix(slot):
-        return jnp.concatenate([full[slot, e] for e in range(nd)], axis=0)
+        return jnp.concatenate([full[slot][e] for e in range(nd)], axis=0)
 
     def fold(value):
         return jnp.sum(value.reshape(block // 8, 8, 128), axis=0)
 
-    correlation, hamilton = split(matrix(0)), split(matrix(1))
+    first = matrix(0)
+    correlation = split(first[:block])
+    hamilton = split(jnp.concatenate([first[block:], matrix(1)], axis=0) if last else matrix(1))
 
     def gradient(r, sums):
         mixed = dot3(correlation, split(gathered(images, r)), NN) + dot3(hamilton, split(gathered(orbs, r)), NN)
@@ -360,9 +371,10 @@
 def on_device(no, nd, orbitals, potential, prev_gradient, prev_direction):
     block, planes, lines, columns = orbitals.shape
     rows = planes * lines
-    chunks = next(n for n in (6, 4, 3, 2, 1) if block % (8 * n) == 0)
+    chunks = next(n for n in (3, 2, 1) if block % (8 * n) == 0)
     nx = no // 2
-    share = block // nd
+    late = block // chunks
+    early = 2 * block - late
     f32 = jnp.float32
     dma = pltpu.SemaphoreType.DMA
     turned = orbitals.reshape(block, rows, columns).transpose(1, 0, 2)
@@ -384,10 +396,9 @@
             pltpu.VMEM((no, rows, block, columns), f32),
             pltpu.VMEM((2, width * lines, block, columns), f32),
             pltpu.VMEM((rows, block, columns), f32),
-            pltpu.VMEM((2, nd, share, no * block), f32),
-            pltpu.VMEM((2, nd, share, no * block), f32),
-            pltpu.VMEM((2, nd, share, no * block), f32),
-            pltpu.VMEM((block, no * block), f32),
+            *[pltpu.VMEM((nd, early // nd, no * block), f32)] * 3,
+            *[pltpu.VMEM((nd, late // nd, no * block), f32)] * 3,
+            pltpu.VMEM((early, no * block), f32),
             pltpu.VMEM((no, 8, columns), f32),
             pltpu.VMEM((nd, 8, columns), f32),
             dma((2,)),

time: 237 us -> 231 us (0.975)
  Pallas kernels: 219 us -> 213 us
    pallas_call x1, Pallas kernels: 219 us -> 213 us  [on_device(): pl.pallas_call(functools.partial(kernel, (no, nd, planes, lines, block, c...]
where the time goes in v2:
time: 231 us
  Pallas kernels  213 us (92%)
  other arithmetic  10.2 us (4%)
  local copies, waits for them, and re-layouts  5.38 us (2%)
  between operations  2.63 us (1%)
    pallas_call x1, Pallas kernels, on_device(): pl.pallas_call(functools.partial(kernel, (no, nd, planes, lines, block, c...  213 us
    add x1, other arithmetic, on_device(): return (orbitals + step_length * direction, direction, grad)  8.81 us
    unnamed x3, local copies, waits for them, and re-layouts  5.38 us

profile of v2, /device:TPU:0, one launch (start us, length us, event | category | flops | bytes accessed | tf_op | source)
XLA Modules:
  0.0 231.2 jit_solution(8266795141008125905)
XLA Ops:
  0.6 5.4 %copy.7 = f32[192,4,8,128]{3,0,2,1:T(8,128)} copy(f32[192,4,8,128]{3,2,1,0:T(8,128)} %param.4) | data formatting | bytes 6291456 | tf_op args[0]
  6.0 0.0 copy-start
  6.0 213.0 %shard_map.67 = (f32[32,192,128]{2,1,0:T(8,128)}, f32[8,128]{1,0:T(8,128)}) custom-call(f32[32,192,128]{2,1,0:T(8,128)} %bitcast.7, f32[32,1,128]{2,1,0:T(1,128)} %bitcast.9, f32[192,4,8,128]{3,2,1,0:T(8,128)} %pg_hbm.1), custom_call_target="tpu_custom_call" | custom-call | tf_op jit(solution)/shard_map/pallas_call | solution.py:382
  219.0 1.4 slice_reduce_fusion
  222.4 0.0 copy-done
  222.4 8.8 %multiply_add_fusion = (f32[192,4,8,128]{3,2,1,0:T(8,128)}, f32[192,4,8,128]{3,2,1,0:T(8,128)}, f32[192,4,8,128]{3,2,1,0:T(8,128)}) fusion(f32[192,4,8,128]{3,2,1,0:T(8,128)S(1)} %copy-done, f32[192,4,8,128]{3,2,1,0:T(8,128)} %param.7, f32[]{:T(128)S(6)} %div.3, f32[192,4,8,128]{3,0,2,1:T(8,128)} %bitcast.8), kind=kLoop, calls=%fused_computation | loop fusion | flops 3932160 | bytes 18874372 | tf_op jit(solution)/shard_map/add | solution.py:419
Async XLA Ops:
  6.0 216.4 %copy-start = (f32[192,4,8,128]{3,2,1,0:T(8,128)S(1)}, f32[192,4,8,128]{3,2,1,0:T(8,128)}, u32[]{:S(2)}) copy-start(f32[192,4,8,128]{3,2,1,0:T(8,128)} %param.4) | copy-start | bytes 9437188

commit v3 on v2

--- a/solution.py
+++ b/solution.py
@@ -113,8 +113,6 @@
             forward(buf, send_f, recv_f, c, j).start()
 
     start_halo(0)
-    if chunks > 1:
-        start_halo(1)
     for c in range(chunks):
         start_spread(orbs, c_s, c_r, c)
 
@@ -167,6 +165,7 @@
         def _():
             down(c).wait_recv()
 
+        start_halo(c + 1)
         stencil(c)
         start_spread(images, i_s, i_r, c)
         pass_on(orbs, c_r, cf_s, cf_r, c)
@@ -231,10 +230,6 @@
             share_out(slot, j).wait_recv()
 
     def early(c, carry):
-        @pl.when(c + 2 < chunks)
-        def _():
-            start_halo(c + 2)
-
         step(c)
 
         @pl.when(c > 0)

time: 231 us -> 231 us (level)
  no operation moved by 1% of the time
where the time goes in v3:
time: 231 us
  Pallas kernels  213 us (92%)
  other arithmetic  10.2 us (4%)
  local copies, waits for them, and re-layouts  5.38 us (2%)
  between operations  2.63 us (1%)
    pallas_call x1, Pallas kernels, on_device(): pl.pallas_call(functools.partial(kernel, (no, nd, planes, lines, block, c...  213 us
    add x1, other arithmetic, on_device(): return (orbitals + step_length * direction, direction, grad)  8.81 us
    unnamed x3, local copies, waits for them, and re-layouts  5.38 us

profile of v3, /device:TPU:0, one launch (start us, length us, event | category | flops | bytes accessed | tf_op | source)
XLA Modules:
  0.0 230.8 jit_solution(17214286319375636110)
XLA Ops:
  0.6 5.4 %copy.7 = f32[192,4,8,128]{3,0,2,1:T(8,128)} copy(f32[192,4,8,128]{3,2,1,0:T(8,128)} %param.4) | data formatting | bytes 6291456 | tf_op args[0]
  6.0 0.0 copy-start
  6.0 212.5 %shard_map.67 = (f32[32,192,128]{2,1,0:T(8,128)}, f32[8,128]{1,0:T(8,128)}) custom-call(f32[32,192,128]{2,1,0:T(8,128)} %bitcast.7, f32[32,1,128]{2,1,0:T(1,128)} %bitcast.9, f32[192,4,8,128]{3,2,1,0:T(8,128)} %pg_hbm.1), custom_call_target="tpu_custom_call" | custom-call | tf_op jit(solution)/shard_map/pallas_call | solution.py:377
  218.6 1.4 slice_reduce_fusion
  222.0 0.0 copy-done
  222.0 8.8 %multiply_add_fusion = (f32[192,4,8,128]{3,2,1,0:T(8,128)}, f32[192,4,8,128]{3,2,1,0:T(8,128)}, f32[192,4,8,128]{3,2,1,0:T(8,128)}) fusion(f32[192,4,8,128]{3,2,1,0:T(8,128)S(1)} %copy-done, f32[192,4,8,128]{3,2,1,0:T(8,128)} %param.7, f32[]{:T(128)S(6)} %div.3, f32[192,4,8,128]{3,0,2,1:T(8,128)} %bitcast.8), kind=kLoop, calls=%fused_computation | loop fusion | flops 3932160 | bytes 18874372 | tf_op jit(solution)/shard_map/add | solution.py:414
Async XLA Ops:
  6.0 216.0 %copy-start = (f32[192,4,8,128]{3,2,1,0:T(8,128)S(1)}, f32[192,4,8,128]{3,2,1,0:T(8,128)}, u32[]{:S(2)}) copy-start(f32[192,4,8,128]{3,2,1,0:T(8,128)} %param.4) | copy-start | bytes 9437188
